TPU v7x, 256 devices: a whole 4x4x8 slice. The times are simulated.
256 devices in a mesh: row: 16 (over y, x), col: 16 (over z, core).
Axes of the slice: x: 4, y: 4, z: 8, core: 2. Of those that a mesh axis runs over, the one named last changes fastest.
Arguments:
- gradients: float32 [2, 8192, 28672], P(None, 'row', 'col'), may hold values from -8 to 8
- sketch: float32 [28672, 256], P('col'), may hold values from -0.03125 to 0.03125
Outputs:
- projection_basis: float32 [2, 8192, 256], P(None, ('row', 'col'))
- projected: float32 [2, 256, 28672], P(None, 'row', 'col')
All inputs are finite; a program needn't handle non-finite values.
Results may differ from a plain program's by a relative error of at most 0.0039.
Values sent between devices are 32-bit elements; how exact they have to be, the bound alone decides.
No kernel may reach another device: no remote copies, remote signals or barrier semaphores. Data moves between devices by JAX's collectives and lax.ppermute only.
A program may use at most 256 MiB of HBM per device.

v0:
```python
import jax
import jax.numpy as jnp
from jax import lax
from jax.sharding import PartitionSpec as P

PRECISE = lax.Precision.HIGHEST


def gram_of(rows):
    return jnp.einsum("bmr,bms->brs", rows, rows, precision=PRECISE)


def lower_solve(lower_factor, rows):

    def single(triangle, block_rows):
        return jax.scipy.linalg.solve_triangular(triangle, block_rows.T, lower=True).T

    return jax.vmap(single)(lower_factor, rows)


def apply_factor(rows, total_gram):
    lower_factor = jnp.linalg.cholesky(total_gram)
    return (lower_solve(lower_factor, rows), jnp.swapaxes(lower_factor, 1, 2))


def factorize(partial_value):
    share = partial_value.shape[1] // lax.axis_size("col")
    summed = lax.psum(partial_value, "col")

    def row_total(rows):
        return lax.psum(gram_of(rows), "row")

    first, unused = apply_factor(summed, row_total(summed))
    whole, unused = apply_factor(first, row_total(first))
    mine = lax.dynamic_slice_in_dim(whole, lax.axis_index("col") * share, share, 1)
    return (whole, mine)


def shards(gradients, sketch):
    total_rows = gradients.shape[1] * lax.axis_size("row")
    partial_value = jnp.einsum("bmn,nr->bmr", gradients, sketch, precision=PRECISE)
    basis_one, unused = factorize(partial_value)
    pulled = lax.psum(jnp.einsum("bmn,bmr->bnr", gradients, basis_one, precision=PRECISE), "row")
    second = jnp.einsum("bmn,bnr->bmr", gradients, pulled, precision=PRECISE)
    basis_two, basis_mine = factorize(second)
    terms = jnp.einsum("bmr,bmn->brn", basis_two, gradients, precision=PRECISE)
    projected = lax.psum_scatter(terms, "row", scatter_dimension=1, tiled=True)
    scale = jnp.sqrt(jnp.float32(total_rows))
    return (basis_mine * scale, projected)


def solution(mesh):
    in_specs = (P(None, "row", "col"), P("col", None))
    out_specs = (P(None, ("row", "col"), None), P(None, "row", "col"))
    return jax.shard_map(shards, mesh=mesh, in_specs=in_specs, out_specs=out_specs, check_vma=False)
```

profile of v0, /device:TPU:1, one launch (start us, length us, event | category | flops | bytes accessed | tf_op | source)
XLA Modules:
  0.0 1394.3 jit_solution(2475704078609199572)
XLA Ops:
  17.7 115.3 %all-reduce.9.cloned.1.call-done = f32[2,512,256]{2,1,0:T(8,128)} async-done(((f32[2,512,256]{2,1,0:T(8,128)}), f32[2,512,256]{2,1,0:T(8,128)}) %all-reduce.9.cloned.1.call-update) | async-done | bytes 1048592 | tf_op jit(solution)/shard_map/psum | solution.py:28
  137.6 94.2 %all-reduce.11.cloned.1.call-done = f32[2,256,256]{1,2,0:T(8,128)} async-done(((f32[2,256,256]{1,2,0:T(8,128)}), f32[2,256,256]{1,2,0:T(8,128)}) %all-reduce.11.cloned.1.call-update) | async-done | bytes 524304 | tf_op jit(solution)/shard_map/psum | solution.py:31
  235.0 23.5 %custom-call.25 = f32[2,128,128]{2,1,0:T(8,128)S(1)} custom-call(f32[2,128,128]{2,1,0:T(8,128)S(1)} %cholesky.350), custom_call_target="Cholesky" | custom-call | tf_op jit(solution)/shard_map/jit(cholesky)/cholesky | solution.py:22
  259.1 20.3 %custom-call.26 = f32[2,1,128,128]{2,3,1,0:T(8,128)} custom-call(f32[2,1,128,128]{3,2,1,0:T(8,128)S(1)} %select_bitcast_fusion.3), custom_call_target="InvertDiagBlocksLowerTriangular" | custom-call | tf_op jit(solution)/shard_map/jit(cholesky)/cholesky | solution.py:22
  283.5 24.9 %custom-call.27 = f32[2,128,128]{2,1,0:T(8,128)} custom-call(f32[2,128,128]{2,1,0:T(8,128)} %convolution_subtract_fusion.7), custom_call_target="Cholesky" | custom-call | tf_op jit(solution)/shard_map/jit(cholesky)/cholesky | solution.py:22
  317.6 41.1 %custom-call.28 = f32[2,2,128,128]{2,3,1,0:T(8,128)} custom-call(f32[2,2,128,128]{3,2,1,0:T(8,128)} %bitcast.171), custom_call_target="InvertDiagBlocksLowerTriangular" | custom-call | tf_op jit(solution)/shard_map/vmap(jit(_solve_triangular))/triangular_solve | solution.py:16
  365.8 94.8 %all-reduce.13.cloned.1.call-done = f32[2,256,256]{1,2,0:T(8,128)} async-done(((f32[2,256,256]{1,2,0:T(8,128)}), f32[2,256,256]{1,2,0:T(8,128)}) %all-reduce.13.cloned.1.call-update) | async-done | bytes 524304 | tf_op jit(solution)/shard_map/psum | solution.py:31
  463.7 23.5 %custom-call.29 = f32[2,128,128]{2,1,0:T(8,128)S(1)} custom-call(f32[2,128,128]{2,1,0:T(8,128)S(1)} %cholesky.353), custom_call_target="Cholesky" | custom-call | tf_op jit(solution)/shard_map/jit(cholesky)/cholesky | solution.py:22
  489.5 21.1 %custom-call.30 = f32[2,1,128,128]{2,3,1,0:T(8,128)} custom-call(f32[2,1,128,128]{3,2,1,0:T(8,128)} %select_bitcast_fusion.2), custom_call_target="InvertDiagBlocksLowerTriangular" | custom-call | tf_op jit(solution)/shard_map/jit(cholesky)/cholesky | solution.py:22
  513.8 24.9 %custom-call.31 = f32[2,128,128]{2,1,0:T(8,128)} custom-call(f32[2,128,128]{2,1,0:T(8,128)} %convolution_subtract_fusion.6), custom_call_target="Cholesky" | custom-call | tf_op jit(solution)/shard_map/jit(cholesky)/cholesky | solution.py:22
  548.5 40.9 %custom-call.32 = f32[2,2,128,128]{2,3,1,0:T(8,128)} custom-call(f32[2,2,128,128]{3,2,1,0:T(8,128)} %bitcast.172), custom_call_target="InvertDiagBlocksLowerTriangular" | custom-call | tf_op jit(solution)/shard_map/vmap(jit(_solve_triangular))/triangular_solve | solution.py:16
  603.8 109.6 %all-reduce.15.cloned.1.call-done = f32[2,1792,256]{1,2,0:T(8,128)} async-done(((f32[2,1792,256]{1,2,0:T(8,128)}), f32[2,1792,256]{1,2,0:T(8,128)}) %all-reduce.15.cloned.1.call-update) | async-done | bytes 3670032 | tf_op jit(solution)/shard_map/psum | solution.py:43
  724.5 111.3 %all-reduce.17.cloned.1.call-done = f32[2,512,256]{1,2,0:T(8,128)} async-done(((f32[2,512,256]{1,2,0:T(8,128)}), f32[2,512,256]{1,2,0:T(8,128)}) %all-reduce.17.cloned.1.call-update) | async-done | bytes 1048592 | tf_op jit(solution)/shard_map/psum | solution.py:28
  839.8 94.0 %all-reduce.19.cloned.1.call-done = f32[2,256,256]{1,2,0:T(8,128)} async-done(((f32[2,256,256]{1,2,0:T(8,128)}), f32[2,256,256]{1,2,0:T(8,128)}) %all-reduce.19.cloned.1.call-update) | async-done | bytes 524304 | tf_op jit(solution)/shard_map/psum | solution.py:31
  937.1 23.5 %custom-call.33 = f32[2,128,128]{2,1,0:T(8,128)S(1)} custom-call(f32[2,128,128]{2,1,0:T(8,128)S(1)} %cholesky.356), custom_call_target="Cholesky" | custom-call | tf_op jit(solution)/shard_map/jit(cholesky)/cholesky | solution.py:22
  962.8 21.1 %custom-call.34 = f32[2,1,128,128]{2,3,1,0:T(8,128)} custom-call(f32[2,1,128,128]{3,2,1,0:T(8,128)} %select_bitcast_fusion.1), custom_call_target="InvertDiagBlocksLowerTriangular" | custom-call | tf_op jit(solution)/shard_map/jit(cholesky)/cholesky | solution.py:22
  987.1 24.9 %custom-call.35 = f32[2,128,128]{2,1,0:T(8,128)} custom-call(f32[2,128,128]{2,1,0:T(8,128)} %convolution_subtract_fusion.5), custom_call_target="Cholesky" | custom-call | tf_op jit(solution)/shard_map/jit(cholesky)/cholesky | solution.py:22
  1021.1 40.9 %custom-call.36 = f32[2,2,128,128]{2,3,1,0:T(8,128)} custom-call(f32[2,2,128,128]{3,2,1,0:T(8,128)} %bitcast.173), custom_call_target="InvertDiagBlocksLowerTriangular" | custom-call | tf_op jit(solution)/shard_map/vmap(jit(_solve_triangular))/triangular_solve | solution.py:16
  1068.6 94.9 %all-reduce.21.cloned.1.call-done = f32[2,256,256]{1,2,0:T(8,128)} async-done(((f32[2,256,256]{1,2,0:T(8,128)}), f32[2,256,256]{1,2,0:T(8,128)}) %all-reduce.21.cloned.1.call-update) | async-done | bytes 524304 | tf_op jit(solution)/shard_map/psum | solution.py:31
  1166.7 23.5 %custom-call.37 = f32[2,128,128]{2,1,0:T(8,128)S(1)} custom-call(f32[2,128,128]{2,1,0:T(8,128)S(1)} %cholesky.359), custom_call_target="Cholesky" | custom-call | tf_op jit(solution)/shard_map/jit(cholesky)/cholesky | solution.py:22
  1192.4 21.1 %custom-call.38 = f32[2,1,128,128]{2,3,1,0:T(8,128)} custom-call(f32[2,1,128,128]{3,2,1,0:T(8,128)} %select_bitcast_fusion), custom_call_target="InvertDiagBlocksLowerTriangular" | custom-call | tf_op jit(solution)/shard_map/jit(cholesky)/cholesky | solution.py:22
  1216.7 24.9 %custom-call.39 = f32[2,128,128]{2,1,0:T(8,128)} custom-call(f32[2,128,128]{2,1,0:T(8,128)} %convolution_subtract_fusion.4), custom_call_target="Cholesky" | custom-call | tf_op jit(solution)/shard_map/jit(cholesky)/cholesky | solution.py:22
  1251.5 40.9 %custom-call.40 = f32[2,2,128,128]{2,3,1,0:T(8,128)} custom-call(f32[2,2,128,128]{3,2,1,0:T(8,128)} %bitcast.170), custom_call_target="InvertDiagBlocksLowerTriangular" | custom-call | tf_op jit(solution)/shard_map/vmap(jit(_solve_triangular))/triangular_solve | solution.py:16
  1307.6 79.7 %reduce-scatter.2.cloned.1.call-done = f32[2,16,1792]{2,1,0:T(8,128)} async-done(((f32[2,256,1792]{2,1,0:T(8,128)}), f32[2,16,1792]{2,1,0:T(8,128)}) %reduce-scatter.2.cloned.1.call-update) | async-done | bytes 229392 | tf_op jit(solution)/shard_map/reduce_scatter | solution.py:47
  (160 shorter events, 166.6 us)
Async XLA Ops:
  7.2 1.5 copy-start
  7.2 125.8 %all-reduce.9.cloned.1.call-start = ((), (), s32[]{:S(2)}) async-start(), calls=%async_computation.1 | async-start | bytes 2097152 | tf_op jit(solution)/shard_map/psum | solution.py:28
  17.6 214.2 %all-reduce.11.cloned.1.call-start = ((), (), s32[]{:S(2)}) async-start(), calls=%async_computation.2 | async-start | bytes 1048576 | tf_op jit(solution)/shard_map/psum | solution.py:31
  133.0 225.8 %copy-start.1 = (f32[2,512,256]{2,1,0:T(8,128)S(1)}, f32[2,512,256]{2,1,0:T(8,128)}, u32[]{:S(2)}) copy-start(f32[2,512,256]{2,1,0:T(8,128)} %all-reduce.9.cloned.1.call-done) | copy-start | bytes 3145732
  137.3 323.3 %all-reduce.13.cloned.1.call-start = ((), (), s32[]{:S(2)}) async-start(), calls=%async_computation.3 | async-start | bytes 1048576 | tf_op jit(solution)/shard_map/psum | solution.py:31
  234.2 0.8 copy-start.12
  309.4 0.8 copy-start.10
  317.6 41.1 %copy-start.4 = (f32[2,256,256]{2,1,0:T(8,128)}, f32[2,256,256]{2,1,0:T(8,128)S(1)}, u32[]{:S(2)}) copy-start(f32[2,256,256]{2,1,0:T(8,128)S(1)} %get-tuple-element.296) | copy-start | bytes 1572868
  365.8 347.7 %all-reduce.15.cloned.1.call-start = ((), (), s32[]{:S(2)}) async-start(), calls=%async_computation.4 | async-start | bytes 7340032 | tf_op jit(solution)/shard_map/psum | solution.py:43
  462.9 0.8 copy-start.13
  539.7 0.8 copy-start.7
  547.7 0.8 copy-start.5
  603.8 232.0 %all-reduce.17.cloned.1.call-start = ((), (), s32[]{:S(2)}) async-start(), calls=%async_computation.5 | async-start | bytes 2097152 | tf_op jit(solution)/shard_map/psum | solution.py:28
  724.5 209.4 %all-reduce.19.cloned.1.call-start = ((), (), s32[]{:S(2)}) async-start(), calls=%async_computation.6 | async-start | bytes 1048576 | tf_op jit(solution)/shard_map/psum | solution.py:31
  835.8 226.3 %copy-start.2 = (f32[2,512,256]{1,2,0:T(8,128)S(1)}, f32[2,512,256]{1,2,0:T(8,128)}, u32[]{:S(2)}) copy-start(f32[2,512,256]{1,2,0:T(8,128)} %all-reduce.17.cloned.1.call-done) | copy-start | bytes 3145732
  839.4 324.1 %all-reduce.21.cloned.1.call-start = ((), (), s32[]{:S(2)}) async-start(), calls=%async_computation.7 | async-start | bytes 1048576 | tf_op jit(solution)/shard_map/psum | solution.py:31
  936.2 0.8 copy-start.14
  960.5 0.7 copy-start.18
  1013.0 0.8 copy-start.8
  1021.1 40.9 %copy-start.6 = (f32[2,256,256]{2,1,0:T(8,128)}, f32[2,256,256]{2,1,0:T(8,128)S(1)}, u32[]{:S(2)}) copy-start(f32[2,256,256]{2,1,0:T(8,128)S(1)} %get-tuple-element.298) | copy-start | bytes 1572868
  1068.6 318.7 %reduce-scatter.2.cloned.1.call-start = ((), (), s32[]{:S(2)}) async-start(), calls=%async_computation.8 | async-start | bytes 3899392 | tf_op jit(solution)/shard_map/reduce_scatter | solution.py:47
  1165.9 0.8 copy-start.11
  1242.6 0.8 copy-start.9
  1250.7 0.8 copy-start.3
  (3 other events, 2.0 us)
Sparse Core Ops, SparseCore 0:
  17.8 115.1 all-reduce.8
  137.4 94.3 all-reduce.10
  365.9 94.6 all-reduce.12
  603.9 109.4 all-reduce.14
  724.6 111.1 all-reduce.16
  839.5 94.3 all-reduce.18
  1068.7 94.7 all-reduce.20
  1306.8 80.3 reduce-scatter.1
where the time goes:
time: 1400 us; the launch traced here: 1390 us
  waiting for transfers between devices  794 us (57%)
  other arithmetic  457 us (33%)
  matrix products  82.6 us (6%)
  local copies, waits for them, and re-layouts  45.1 us (3%)
  between operations  14.7 us (1%)
    psum x4, waiting for transfers between devices, row_total(): return lax.psum(gram_of(rows), 'row')  378 us
    another operation x33, other arithmetic, apply_factor(): lower_factor = jnp.linalg.cholesky(total_gram)  284 us
    psum x2, waiting for transfers between devices, factorize(): summed = lax.psum(partial_value, 'col')  227 us
    another operation x10, other arithmetic, single(): jax.scipy.linalg.solve_triangular(triangle, block_rows.T, lower=True)  169 us
    psum x1, waiting for transfers between devices, shards(): lax.psum(jnp.einsum('bmn,bmr->bnr', gradients, basis_one, precision=PRECI...  110 us
    reduce_scatter x1, waiting for transfers between devices, shards(): projected = lax.psum_scatter(terms, 'row', scatter_dimension=1, tiled=True)  79.7 us
  transfers between devices with their start and end apart: 8, of which 8 were waited for; matrix products, arithmetic and copies ran while one was open for 0% of the time, Pallas kernels for 0%

commit v1 on v0

v1 whole, which is shorter than its diff:
```python
import jax
import jax.numpy as jnp
from jax import lax
from jax.experimental import pallas as pl
from jax.experimental.pallas import tpu as pltpu
from jax.sharding import PartitionSpec as P

FULL = lax.Precision.HIGHEST
FAST = lax.Precision.HIGH
CORES = 2
PANEL = 32


def inverse_factor_kernel(gram_ref, out_ref, work_ref):
    grads, rank, _ = gram_ref.shape
    for g in range(grads):
        work_ref[g] = gram_ref[g]
    rows = lax.broadcasted_iota(jnp.int32, (PANEL, rank), 0)
    cols = lax.broadcasted_iota(jnp.int32, (PANEL, rank), 1)
    for lo in range(0, rank, PANEL):
        hi = lo + PANEL
        left = [work_ref[g, lo:hi, :] for g in range(grads)]
        right = [jnp.where(cols == rows + lo, 1.0, 0.0) for g in range(grads)]
        for k in range(PANEL):
            for g in range(grads):
                column = left[g][:, lo + k:lo + k + 1]
                inverse = lax.rsqrt(column[k:k + 1, :])
                left_row = left[g][k:k + 1, :] * inverse
                right_row = right[g][k:k + 1, :] * inverse
                factor = column * inverse
                left[g] = jnp.where(rows > k, left[g] - factor * left_row, jnp.where(rows == k, left_row, left[g]))
                right[g] = jnp.where(rows > k, right[g] - factor * right_row, jnp.where(rows == k, right_row, right[g]))
        inside = (cols >= lo) & (cols < hi)
        for g in range(grads):
            whole = jnp.where(inside, right[g], left[g])
            out_ref[g, lo:hi, :] = jnp.where(cols < hi, whole, 0.0)
            if hi < rank:
                update = lax.dot_general(left[g], whole, (((0,), (0,)), ((), ())), precision=FULL, preferred_element_type=jnp.float32)
                places = lax.broadcasted_iota(jnp.int32, (rank - hi, rank), 1)
                kept = jnp.where((places >= lo) & (places < hi), 0.0, work_ref[g, hi:, :])
                work_ref[g, hi:, :] = kept - update[hi:]


def inverse_factor(gram):
    return pl.pallas_call(
        inverse_factor_kernel,
        out_shape=jax.ShapeDtypeStruct(gram.shape, jnp.float32),
        in_specs=[pl.BlockSpec(memory_space=pltpu.VMEM)],
        out_specs=pl.BlockSpec(memory_space=pltpu.VMEM),
        scratch_shapes=[pltpu.VMEM(gram.shape, jnp.float32)],
        compiler_params=pltpu.CompilerParams(vmem_limit_bytes=32 * 2**20),
    )(gram)


def swap_core(value):
    size = lax.axis_size("col")
    return lax.ppermute(value, "col", [(i, i ^ 1) for i in range(size)])


def chips(value):
    size = lax.axis_size("col")
    groups = [list(range(core, size, CORES)) for core in range(CORES)]
    return lax.all_to_all(value, "col", 0, 0, axis_index_groups=groups, tiled=True)


def spread(value, count):
    return jnp.broadcast_to(value[None], (count,) + value.shape)


def both_cores(value, axis):
    other = swap_core(value)
    core = lax.axis_index("col") % CORES
    return jnp.stack([jnp.where(core == 0, value, other), jnp.where(core == 0, other, value)], axis)


def half_sum(value, axis):
    core = lax.axis_index("col") % CORES
    mine = lax.dynamic_index_in_dim(value, core, axis, keepdims=False)
    return mine + swap_core(lax.dynamic_index_in_dim(value, 1 - core, axis, keepdims=False))


def shards(gradients, sketch):
    grads, depth, width = gradients.shape
    rank = sketch.shape[1]
    row_size, col_size = lax.axis_size("row"), lax.axis_size("col")
    chip_count = col_size // CORES
    part = depth // col_size
    slab = width // row_size
    total_rows = depth * row_size

    def halve(value):
        pieces = value.reshape(grads, chip_count, CORES, part, rank)
        return jnp.swapaxes(half_sum(pieces, 2), 0, 1)

    def join(pieces):
        whole = both_cores(pieces, 2)
        return jnp.moveaxis(whole, 0, 1).reshape(grads, depth, rank)

    first_part = jnp.einsum("bmn,nr->bmr", gradients, sketch, precision=FAST)
    first_mine = jnp.sum(chips(halve(first_part)), 0)
    first = join(chips(spread(first_mine, chip_count)))

    pulled_part = jnp.einsum("bmn,bmr->bnr", gradients, first, precision=FAST)
    pulled_part = jnp.swapaxes(pulled_part.reshape(grads, row_size, slab, rank), 0, 1)
    pulled_mine = jnp.sum(lax.all_to_all(pulled_part, "row", 0, 0, tiled=True), 0)
    pulled = lax.all_to_all(spread(pulled_mine, row_size), "row", 0, 0, tiled=True)
    pulled = jnp.swapaxes(pulled, 0, 1).reshape(grads, width, rank)

    second_part = jnp.einsum("bmn,bnr->bmr", gradients, pulled, precision=FAST)
    gram_part = half_sum(jnp.einsum("bnr,bns->brs", pulled, pulled, precision=FULL), 0)
    packed = jnp.concatenate([halve(second_part).reshape(chip_count, grads * part, rank), gram_part.reshape(chip_count, rank // chip_count, rank)], 1)
    packed_mine = jnp.sum(chips(packed), 0)
    packed = chips(spread(packed_mine, chip_count))
    raw = join(packed[:, :grads * part].reshape(chip_count, grads, part, rank))
    gram = both_cores(packed[:, grads * part:].reshape(rank, rank), 0)

    balanced = jnp.einsum("bmr,bsr->bms", raw, inverse_factor(gram), precision=FULL)
    chosen = lax.dynamic_index_in_dim(balanced, lax.axis_index("col") % CORES, 0, keepdims=False)
    gram_part = jnp.einsum("mr,ms->rs", chosen, chosen, precision=FULL)
    gram_part = gram_part.reshape(row_size, rank // row_size, rank)
    gram_mine = jnp.sum(lax.all_to_all(gram_part, "row", 0, 0, tiled=True), 0)
    gram = lax.all_to_all(spread(gram_mine, row_size), "row", 0, 0, tiled=True).reshape(rank, rank)
    gram = both_cores(gram, 0)
    basis = jnp.einsum("bmr,bsr->bms", balanced, inverse_factor(gram), precision=FULL)

    terms = jnp.einsum("bmr,bmn->brn", basis, gradients, precision=FAST)
    terms = jnp.swapaxes(terms.reshape(grads, row_size, rank // row_size, width), 0, 1)
    projected = jnp.sum(lax.all_to_all(terms, "row", 0, 0, tiled=True), 0)
    basis_mine = lax.dynamic_slice_in_dim(basis, lax.axis_index("col") * part, part, 1)
    return (basis_mine * jnp.sqrt(jnp.float32(total_rows)), projected)


def solution(mesh):
    in_specs = (P(None, "row", "col"), P("col", None))
    out_specs = (P(None, ("row", "col"), None), P(None, "row", "col"))
    return jax.shard_map(shards, mesh=mesh, in_specs=in_specs, out_specs=out_specs, check_vma=False)
```

time: 1400 us -> 416 us (0.30)
  waiting for transfers between devices: 794 us -> 61.2 us
  other arithmetic: 457 us -> 7.74 us
  blocking collectives: 0 us -> 212 us
  Pallas kernels: 0 us -> 50.2 us
  matrix products: 82.6 us -> 35.7 us
  local copies, waits for them, and re-layouts: 45.1 us -> 23.3 us
  starting transfers between devices: 0.91 us -> 17.4 us
    psum x7 -> x0, waiting for transfers between devices: 714 us -> none  [the longest x4 378 us: row_total(): return lax.psum(gram_of(rows), 'row')]
    another operation x43 -> x7, other arithmetic: 453 us -> 0.48 us  [both_cores(): jnp.stack([jnp.where(core == 0, value, other), jnp.where(core == 0, other...]
    all_to_all x0 -> x8, blocking collectives: none -> 212 us  [the longest x4 92.1 us: chips(): lax.all_to_all(value, 'col', 0, 0, axis_index_groups=groups, tiled=True)]
    reduce_scatter x1 -> x0, waiting for transfers between devices: 79.7 us -> none  [shards(): projected = lax.psum_scatter(terms, 'row', scatter_dimension=1, tiled=True)]
    all_to_all x0 -> x1, waiting for transfers between devices: none -> 54.2 us  [shards(): projected = jnp.sum(lax.all_to_all(terms, 'row', 0, 0, tiled=True), 0)]
    pallas_call x0 -> x2, Pallas kernels: none -> 50.2 us  [inverse_factor(): pl.pallas_call(inverse_factor_kernel, out_shape=jax.ShapeDtypeStruct(gram...]
    another operation x20 -> x0, matrix products: 31.4 us -> none  [the longest x12 18.7 us: single(): jax.scipy.linalg.solve_triangular(triangle, block_rows.T, lower=True)]
    another operation x37 -> x0, local copies, waits for them, and re-layouts: 28.3 us -> none  [the longest x29 24.5 us: single(): jax.scipy.linalg.solve_triangular(triangle, block_rows.T, lower=True)]
  transfers between devices with their start and end apart: 8 -> 8, of which waited for: 8 -> 6; matrix products, arithmetic and copies ran while one was open for 0% -> 0% of each run, Pallas kernels for 0% -> 6%
where the time goes in v1:
time: 416 us; the launch traced here: 409 us
  blocking collectives  212 us (51%)
  waiting for transfers between devices  61.2 us (15%)
  Pallas kernels  50.2 us (12%)
  matrix products  35.7 us (9%)
  local copies, waits for them, and re-layouts  23.3 us (6%)
  starting transfers between devices  17.4 us (4%)
  other arithmetic  7.74 us (2%)
    all_to_all x4, blocking collectives, chips(): lax.all_to_all(value, 'col', 0, 0, axis_index_groups=groups, tiled=True)  92.1 us
    all_to_all x1, waiting for transfers between devices, shards(): projected = jnp.sum(lax.all_to_all(terms, 'row', 0, 0, tiled=True), 0)  54.2 us
    all_to_all x1, blocking collectives, shards(): lax.all_to_all(pulled_part, 'row', 0, 0, tiled=True)  51.1 us
    pallas_call x2, Pallas kernels, inverse_factor(): pl.pallas_call(inverse_factor_kernel, out_shape=jax.ShapeDtypeStruct(gram...  50.2 us
    all_to_all x1, blocking collectives, shards(): lax.all_to_all(spread(pulled_mine, row_size), 'row', 0, 0, tiled=True)  47.4 us
    ppermute x7, starting transfers between devices, swap_core(): return lax.ppermute(value, 'col', [(i, i ^ 1) for i in range(size)])  12.9 us
    all_to_all x1, blocking collectives, shards(): gram_mine = jnp.sum(lax.all_to_all(gram_part, 'row', 0, 0, tiled=True), 0)  11.2 us
    dot_general x1, local copies, waits for them, and re-layouts, shards(): second_part = jnp.einsum('bmn,bnr->bmr', gradients, pulled, precision=FAST)  11 us
  transfers between devices with their start and end apart: 8, of which 6 were waited for; matrix products, arithmetic and copies ran while one was open for 0% of the time, Pallas kernels for 6%

profile of v1, /device:TPU:1, one launch (start us, length us, event | category | flops | bytes accessed | tf_op | source)
XLA Modules:
  0.0 409.1 jit_solution(3176272565179180347)
XLA Ops:
  2.1 5.3 %fusion = f32[2,512,256]{2,1,0:T(8,128)S(1)} fusion(f32[2,512,1792]{2,1,0:T(8,128)} %param.2, f32[1792,256]{1,0:T(8,128)S(1)} %copy-done), kind=kOutput, calls=%fused_computation.2 | convolution fusion | flops 2818572288 | bytes 10223616 | tf_op jit(solution)/shard_map/bmn,nr->bmr/dot_general | solution.py:99
  7.6 3.3 collective-permute-start
  12.5 23.0 %all_to_all.45 = f32[8,2,32,256]{3,2,1,0:T(8,128)S(1)} all-to-all(f32[8,2,32,256]{3,2,1,0:T(8,128)S(1)} %fusion.5), channel_id=1, replica_groups={{0,2,4,6,8,10,12,14},{1,3,5,7,9,11,13,15},{16,18,20,22,24,26,28,30},{17..., dimensions={0} | all-to-all | bytes 1048576 | tf_op jit(solution)/shard_map/all_to_all | solution.py:63
  35.6 17.3 %all_to_all.46 = f32[8,2,32,256]{3,2,1,0:T(8,128)S(1)} all-to-all(f32[8,2,32,256]{3,2,1,0:T(8,128)S(1)} %broadcast_in_dim.8), channel_id=1, replica_groups={{0,2,4,6,8,10,12,14},{1,3,5,7,9,11,13,15},{16,18,20,22,24,26,28,30},{17..., dimensions={0} | all-to-all | bytes 1048576 | tf_op jit(solution)/shard_map/all_to_all | solution.py:63
  52.9 3.7 collective-permute-start.1
  58.3 8.3 %convolution_bitcast_fusion = f32[2,1792,256]{1,2,0:T(8,128)} fusion(f32[2,512,256]{2,1,0:T(8,128)S(1)} %bitcast.106, f32[2,512,1792]{2,1,0:T(8,128)} %param.2), kind=kOutput, calls=%fused_computation.1 | convolution fusion | flops 2818572288 | bytes 12058624 | tf_op jit(solution)/shard_map/bmn,bmr->bnr/dot_general | solution.py:103
  66.7 5.2 %copy.46 = f32[2,1792,256]{2,1,0:T(8,128)} copy(f32[2,1792,256]{1,2,0:T(8,128)} %convolution_bitcast_fusion) | data formatting | bytes 7340032 | tf_op jit(solution)/shard_map/bmn,bmr->bnr/dot_general | solution.py:103
  74.1 51.1 %all_to_all.47 = f32[16,2,112,256]{3,2,1,0:T(8,128)} all-to-all(f32[16,2,112,256]{3,2,1,0:T(8,128)S(1)} %copy.47), channel_id=1, replica_groups=mesh['row'=16,'col'=16] {'row'}, dimensions={0} | all-to-all | bytes 7340032 | tf_op jit(solution)/shard_map/all_to_all | solution.py:105
  127.9 47.4 %all_to_all.48 = f32[16,2,112,256]{3,2,1,0:T(8,128)S(1)} all-to-all(f32[16,2,112,256]{3,2,1,0:T(8,128)S(1)} %broadcast_in_dim.9), channel_id=1, replica_groups=mesh['row'=16,'col'=16] {'row'}, dimensions={0} | all-to-all | bytes 7340032 | tf_op jit(solution)/shard_map/all_to_all | solution.py:106
  175.6 6.2 %fusion.6 = f32[2,256,256]{2,1,0:T(8,128)S(1)} fusion(f32[2,1792,256]{2,1,0:T(8,128)S(1)} %bitcast.98), kind=kOutput, calls=%fused_computation.32 | convolution fusion | flops 2818572288 | bytes 4194304 | tf_op jit(solution)/shard_map/bnr,bns->brs/dot_general | solution.py:110
  181.9 6.2 %convolution_bitcast_fusion.1 = f32[2,512,256]{1,2,0:T(8,128)S(1)} fusion(f32[2,1792,256]{2,1,0:T(8,128)S(1)} %bitcast.99, f32[2,512,1792]{2,1,0:T(8,128)S(1)} %bitcast.97), kind=kOutput, calls=%fused_computation.4 | convolution fusion | flops 2818572288 | bytes 12058624 | tf_op jit(solution)/shard_map/bmn,bnr->bmr/dot_general | solution.py:109
  188.1 11.0 %copy.50 = f32[2,512,256]{2,1,0:T(8,128)S(1)} copy(f32[2,512,256]{1,2,0:T(8,128)S(1)} %convolution_bitcast_fusion.1) | data formatting | bytes 2097152 | tf_op jit(solution)/shard_map/bmn,bnr->bmr/dot_general | solution.py:109
  199.2 2.3 collective-permute-start.2
  203.7 26.0 %all_to_all.49 = f32[8,96,256]{2,1,0:T(8,128)S(1)} all-to-all(f32[8,96,256]{2,1,0:T(8,128)S(1)} %pad_maximum_fusion.1), channel_id=1, replica_groups={{0,2,4,6,8,10,12,14},{1,3,5,7,9,11,13,15},{16,18,20,22,24,26,28,30},{17..., dimensions={0} | all-to-all | bytes 1572864 | tf_op jit(solution)/shard_map/all_to_all | solution.py:63
  229.8 25.9 %all_to_all.50 = f32[8,96,256]{2,1,0:T(8,128)S(1)} all-to-all(f32[8,96,256]{2,1,0:T(8,128)S(1)} %broadcast_in_dim.10), channel_id=1, replica_groups={{0,2,4,6,8,10,12,14},{1,3,5,7,9,11,13,15},{16,18,20,22,24,26,28,30},{17..., dimensions={0} | all-to-all | bytes 1572864 | tf_op jit(solution)/shard_map/all_to_all | solution.py:63
  257.6 25.1 %shard_map.41 = f32[2,256,256]{2,1,0:T(8,128)S(1)} custom-call(f32[2,256,256]{2,1,0:T(8,128)S(1)} %pad_maximum_fusion.2.gram_ref), custom_call_target="tpu_custom_call" | custom-call | tf_op jit(solution)/shard_map/pallas_call | solution.py:45
  284.9 11.2 %all_to_all.51 = f32[16,16,256]{2,1,0:T(8,128)S(1)} all-to-all(f32[16,16,256]{2,1,0:T(8,128)S(1)} %fusion.2), channel_id=1, replica_groups=mesh['row'=16,'col'=16] {'row'}, dimensions={0} | all-to-all | bytes 524288 | tf_op jit(solution)/shard_map/all_to_all | solution.py:121
  296.1 10.1 %all_to_all.52 = f32[16,16,256]{2,1,0:T(8,128)S(1)} all-to-all(f32[16,16,256]{2,1,0:T(8,128)S(1)} %broadcast_in_dim.11), channel_id=1, replica_groups=mesh['row'=16,'col'=16] {'row'}, dimensions={0} | all-to-all | bytes 524288 | tf_op jit(solution)/shard_map/all_to_all | solution.py:122
  306.3 2.7 collective-permute-start.6
  310.2 25.1 %shard_map.42 = f32[2,256,256]{2,1,0:T(8,128)S(1)} custom-call(f32[2,256,256]{2,1,0:T(8,128)S(1)} %pad_maximum_fusion.3.gram_ref), custom_call_target="tpu_custom_call" | custom-call | tf_op jit(solution)/shard_map/pallas_call | solution.py:45
  337.2 6.1 %fusion.9 = f32[2,256,1792]{2,1,0:T(8,128)S(1)} fusion(f32[2,512,256]{2,1,0:T(8,128)S(1)} %fusion.8, f32[2,512,1792]{2,1,0:T(8,128)} %param.2), kind=kOutput, calls=%fused_computation.35 | convolution fusion | flops 2818572288 | bytes 12058624 | tf_op jit(solution)/shard_map/bmr,bmn->brn/dot_general | solution.py:126
  345.4 4.5 %all-to-all-start.8 = ((f32[16,2,16,1792]{3,2,1,0:T(8,128)}), f32[16,2,16,1792]{3,2,1,0:T(8,128)}, u32[]{:S(2)}, u32[]{:S(2)}) async-start(f32[16,2,16,1792]{3,2,1,0:T(8,128)} %bitcast.100), calls=%async_computation.8 | async-start | bytes 7340032 | tf_op jit(solution)/shard_map/all_to_all | solution.py:128
  351.5 54.2 %all-to-all-done.8 = f32[16,2,16,1792]{3,2,1,0:T(8,128)} async-done(((f32[16,2,16,1792]{3,2,1,0:T(8,128)}), f32[16,2,16,1792]{3,2,1,0:T(8,128)}, u32[]{:S(2)}, u32[]{:S(2)}) %all-to-all-start.8) | async-done | bytes 3670048 | tf_op jit(solution)/shard_map/all_to_all | solution.py:128
  405.8 2.9 reduce_sum.49
  (59 shorter events, 23.4 us)
Async XLA Ops:
  0.6 1.5 copy-start
  7.6 4.9 %collective-permute-start = (f32[2,8,32,256]{3,2,0,1:T(8,128)S(1)}, f32[2,8,32,256]{3,2,0,1:T(8,128)S(1)}, u32[]{:S(2)}, u32[]{:S(2)}) collective-permute-start(f32[2,8,32,256]{3,2,0,1:T(8,128)S(1)} %bitcast.115), channel_id=1, source_target_pairs={{0,1},{1,0},{2,3},{3,2},{4,5},{5,4},{6,7},{7,6},{8,9},{9,8},{10,11... | collective-permute-start | bytes 1572872 | tf_op jit(solution)/shard_map/ppermute | solution.py:57
  52.9 5.2 %collective-permute-start.1 = (f32[8,2,32,256]{3,2,0,1:T(8,128)S(1)}, f32[8,2,32,256]{3,2,0,1:T(8,128)S(1)}, u32[]{:S(2)}, u32[]{:S(2)}) collective-permute-start(f32[8,2,32,256]{3,2,0,1:T(8,128)S(1)} %copy.42), channel_id=1, source_target_pairs={{0,1},{1,0},{2,3},{3,2},{4,5},{5,4},{6,7},{7,6},{8,9},{9,8},{10,11... | collective-permute-start | bytes 1572872 | tf_op jit(solution)/shard_map/ppermute | solution.py:57
  175.3 6.5 %slice-start = ((s8[7340032]{0:T(1024)(128)(4,1)}), s8[4194304]{0:T(1024)(128)(4,1)S(1)}, s32[]{:S(2)}) async-start(s8[7340032]{0:T(1024)(128)(4,1)} %bitcast.96), calls=%async_computation.9 | async-start | bytes 8388608
  175.6 6.2 %slice-start.1 = ((s8[7340032]{0:T(1024)(128)(4,1)}), s8[3145728]{0:T(1024)(128)(4,1)S(1)}, s32[]{:S(2)}) async-start(s8[7340032]{0:T(1024)(128)(4,1)} %bitcast.96), calls=%async_computation.10 | async-start | bytes 6291456
  199.2 4.3 %collective-permute-start.2 = (f32[2,8,32,256]{3,2,1,0:T(8,128)S(1)}, f32[2,8,32,256]{3,2,1,0:T(8,128)S(1)}, u32[]{:S(2)}, u32[]{:S(2)}) collective-permute-start(f32[2,8,32,256]{3,2,1,0:T(8,128)S(1)} %dynamic-slice_bitcast_fusion), channel_id=1, source_target_pairs={{0,1},{1,0},{2,3},{3,2},{4,5},{5,4},{6,7},{7,6},{8,9},{9,8},{10,11... | collective-permute-start | bytes 1572872 | tf_op jit(solution)/shard_map/ppermute | solution.py:57
  201.6 1.9 collective-permute-start.3
  255.7 1.8 collective-permute-start.5
  256.5 26.3 %collective-permute-start.4 = (f32[8,2,32,256]{3,2,0,1:T(8,128)S(1)}, f32[8,2,32,256]{3,2,0,1:T(8,128)S(1)}, u32[]{:S(2)}, u32[]{:S(2)}) collective-permute-start(f32[8,2,32,256]{3,2,0,1:T(8,128)S(1)} %copy.54), channel_id=1, source_target_pairs={{0,1},{1,0},{2,3},{3,2},{4,5},{5,4},{6,7},{7,6},{8,9},{9,8},{10,11... | collective-permute-start | bytes 1572872 | tf_op jit(solution)/shard_map/ppermute | solution.py:57
  306.3 3.8 collective-permute-start.6
  337.2 6.1 %copy-start.2 = (f32[2,512,256]{2,1,0:T(8,128)}, f32[2,512,256]{2,1,0:T(8,128)S(1)}, u32[]{:S(2)}) copy-start(f32[2,512,256]{2,1,0:T(8,128)S(1)} %fusion.8) | copy-start | bytes 3145732
  345.4 60.4 %all-to-all-start.8 = ((f32[16,2,16,1792]{3,2,1,0:T(8,128)}), f32[16,2,16,1792]{3,2,1,0:T(8,128)}, u32[]{:S(2)}, u32[]{:S(2)}) async-start(f32[16,2,16,1792]{3,2,1,0:T(8,128)} %bitcast.100), calls=%async_computation.8 | async-start | bytes 7340032 | tf_op jit(solution)/shard_map/all_to_all | solution.py:128
  349.9 58.8 %copy-start.1 = (f32[1792,256]{1,0:T(8,128)S(1)}, f32[1792,256]{1,0:T(8,128)}, u32[]{:S(2)}) copy-start(f32[1792,256]{1,0:T(8,128)} %param.3) | copy-start | bytes 5505028
